TPU v7x, 32 devices: a whole 2x2x4 slice. The times are simulated.
32 devices in a mesh: groups: 2 (over y), seq: 8 (over z, x), mp: 2 (over core).
Axes of the slice: x: 2, y: 2, z: 4, core: 2. Of those that a mesh axis runs over, the one named last changes fastest.
Arguments:
- queries: bfloat16 [32, 5120], P(('groups', 'seq'), 'mp'), parts along dimension 0, may hold values from -40 to 40
- prefix_keys: bfloat16 [4096, 1024], P(('groups', 'seq'), 'mp'), parts along dimension 0, may hold values from -10 to 10
- prefix_values: bfloat16 [4096, 1024], P(('groups', 'seq'), 'mp'), parts along dimension 0, may hold values from -6 to 6
- suffix_keys: bfloat16 [32, 8, 1024], P(('groups', 'seq'), None, 'mp'), parts along dimension 0, may hold values from -7 to 7
- suffix_values: bfloat16 [32, 8, 1024], P(('groups', 'seq'), None, 'mp'), parts along dimension 0, may hold values from -6 to 6
- new_keys: bfloat16 [32, 1024], P(('groups', 'seq'), 'mp'), parts along dimension 0, may hold values from -7 to 7
- new_values: bfloat16 [32, 1024], P(('groups', 'seq'), 'mp'), parts along dimension 0, may hold values from -6 to 6
- suffix_lengths: int32 [32], P(('groups', 'seq')), parts along dimension 0, may hold values from 0 to 7
- fork_list: int32 [16, 2], P(('groups', 'seq')), parts along dimension 0, may hold values from 0 to 15, as said below
Outputs:
- attended: bfloat16 [32, 5120], P(('groups', 'seq'), 'mp'), parts along dimension 0
- cache_keys: bfloat16 [32, 8, 1024], P(('groups', 'seq'), None, 'mp'), parts along dimension 0
- cache_values: bfloat16 [32, 8, 1024], P(('groups', 'seq'), None, 'mp'), parts along dimension 0
There are 2 independent parts, one for each index of `groups`. A program takes and returns all parts, laid end to end along the dimension named above; each array names one. Nothing has to cross between parts.
Inputs may be any that keep to these rules, and one draw needn't show every extreme that they name: `fork_list`: row f has its parent among the branches f * 2 to f * 2 + 1; the children are distinct and none of them is a parent.
All inputs are finite; a program needn't handle non-finite values.
Results may differ from a plain program's by a relative error of at most 0.0044.
Values may be sent and summed in bfloat16 or wider, within the bound.
A program may use at most 64 MiB of HBM per device.

v0:
```python
import functools
import math

import jax
import jax.numpy as jnp
from jax import lax
from jax.experimental import pallas as pl
from jax.experimental.pallas import tpu as pltpu
from jax.sharding import PartitionSpec as P

HQ = 40
KVH = 8
HD = 128
GROUP = HQ // KVH
BRANCHES = 2
TILE = 8
MESH = pl.DeviceIdType.MESH
NT = (((1,), (1,)), ((), ()))
UNROLL_UP_TO = 16
F32 = jnp.float32
BF16 = jnp.bfloat16


def each(start, stop, body):
    if stop - start <= UNROLL_UP_TO:
        for index in range(start, stop):
            body(index)
    else:
        def step(index, carry):
            body(index)
            return carry

        lax.fori_loop(start, stop, step, 0)


def fold(start, stop, body, carry):
    if stop - start <= UNROLL_UP_TO:
        for index in range(start, stop):
            carry = body(index, carry)
        return carry
    return lax.fori_loop(start, stop, body, carry)


def kernel(
    n,
    q_hbm, pk_hbm, pv_hbm, sk_hbm, sv_hbm, nk_hbm, nv_hbm, len_ref, fork_ref,
    att, ck, cv,
    q_in, pk, pv, sk, sv, nk, nv,
    q_f32, q_tiles, pieces, res_out, res_in, att_rows,
    in_sem, q_send, q_recv, p_send, p_recv, r_send, r_recv,
):
    me = lax.axis_index("seq")
    slots = sk.shape[1]
    kv_local = pk.shape[1] // HD
    scale = 1.0 / math.sqrt(HD)
    base = me * BRANCHES
    rest = kv_local * TILE
    notes_at = rest + TILE
    chunk = math.gcd(n, 4)

    def partner(k):
        other, bit = me, 1
        while bit < n:
            other = other + (k // bit) % 2 * bit * (1 - 2 * ((me // bit) % 2))
            bit *= 2
        return {"seq": other}

    barrier = pltpu.get_barrier_semaphore()
    each(1, n, lambda k: pl.semaphore_signal(
        barrier, inc=1, device_id=partner(k), device_id_type=MESH))

    loads = [
        pltpu.make_async_copy(src, dst, in_sem.at[i])
        for i, (src, dst) in enumerate([
            (q_hbm, q_in), (sk_hbm, sk), (sv_hbm, sv), (pk_hbm, pk),
            (pv_hbm, pv), (nk_hbm, nk), (nv_hbm, nv)])
    ]
    for load in loads:
        load.start()

    def row_of(g, h):
        return g * TILE + h * BRANCHES if h < GROUP - 1 else rest + g * BRANCHES

    parent = fork_ref[0, 0] - base
    parent_length = jnp.where(parent == 0, len_ref[0], len_ref[1])
    q_f32[notes_at:] = jnp.zeros((TILE, HD), F32)
    q_f32[notes_at:notes_at + 1] = jnp.full((1, HD), fork_ref[0, 1].astype(F32))
    q_f32[notes_at + 1:notes_at + 2] = jnp.full((1, HD), parent_length.astype(F32))
    loads[0].wait()
    q_all = q_in[...].astype(F32)
    for g in range(kv_local):
        for h in range(GROUP):
            at = (g * GROUP + h) * HD
            q_f32[row_of(g, h):row_of(g, h) + BRANCHES, :] = q_all[:, at:at + HD]
    q_tiles[0] = q_f32[...].astype(BF16)

    pl.semaphore_wait(barrier, n - 1)

    def copy(src, dst, send, recv, k):
        return pltpu.make_async_remote_copy(
            src_ref=src, dst_ref=dst, send_sem=send.at[k], recv_sem=recv.at[k],
            device_id=partner(k), device_id_type=MESH)

    def q_copy(k):
        return copy(q_tiles.at[0], q_tiles.at[k], q_send, q_recv, k)

    def p_copy(k):
        return copy(pieces.at[0], pieces.at[k], p_send, p_recv, k)

    def r_copy(k):
        return copy(res_out.at[k], res_in.at[k], r_send, r_recv, k)

    def far_first(body):
        each(chunk, n, body)
        each(1, chunk, body)

    far_first(lambda k: q_copy(k).start())

    loads[1].wait()
    loads[2].wait()

    def own_suffix(j):
        return jnp.concatenate([sk[j].astype(F32), sv[j].astype(F32)], axis=0)

    parent_b = jnp.full((2 * slots, sk.shape[2]), parent.astype(F32))
    pieces[0] = jnp.where(parent_b == 0.0, own_suffix(0), own_suffix(1)).astype(BF16)
    far_first(lambda k: p_copy(k).start())

    loads[3].wait()
    loads[4].wait()

    count = chunk * TILE
    lane = lax.rem(lax.broadcasted_iota(jnp.int32, (count, HD), 1), 16)
    owner_s = lax.rem(lax.broadcasted_iota(jnp.int32, (count, pk.shape[0]), 0), TILE) // BRANCHES
    owner_o = lax.rem(lax.broadcasted_iota(jnp.int32, (count, HD), 0), TILE) // BRANCHES

    def softmax(scores):
        row_max = jnp.max(scores, axis=1, keepdims=True)
        weights = jnp.exp(scores - row_max)
        return row_max, jnp.sum(weights, axis=1, keepdims=True), weights.astype(BF16)

    def block(first):
        tiles = q_tiles[pl.ds(first, chunk)].astype(F32)

        def rows(at):
            return tiles[:, at:at + TILE].reshape(count, HD)

        last = rows(rest)
        scores, rest_scores = [], None
        for g in range(kv_local):
            q = jnp.concatenate([rows(g * TILE), last], axis=0).astype(BF16)
            s = lax.dot_general(
                q, pk[:, g * HD:(g + 1) * HD], NT, preferred_element_type=F32) * scale
            scores.append(s[:count])
            rest_scores = s[count:] if g == 0 else jnp.where(owner_s == g, s[count:], rest_scores)
        outputs = []
        top = jnp.zeros((count, HD), F32)
        total = jnp.ones((count, HD), F32)
        for g, s in enumerate(scores + [rest_scores]):
            row_max, row_total, weights = softmax(s)
            if g < kv_local:
                summed = jnp.dot(
                    weights, pv[:, g * HD:(g + 1) * HD], preferred_element_type=F32)
            else:
                every = jnp.dot(weights, pv[...], preferred_element_type=F32)
                summed = every[:, :HD]
                for i in range(1, kv_local):
                    summed = jnp.where(owner_o == i, every[:, i * HD:(i + 1) * HD], summed)
            outputs.append(summed * (1.0 / row_total))
            top = jnp.where(lane == g, row_max, top)
            total = jnp.where(lane == g, row_total, total)
        lse = top + jnp.log(total)
        high = lse.astype(BF16).astype(F32)
        middle = (lse - high).astype(BF16).astype(F32)
        low = lse - high - middle
        at = lax.broadcasted_iota(jnp.int32, (count, HD), 1) // 16
        outputs.append(jnp.where(at == 0, high, jnp.where(at == 1, middle, low)))
        res_out[pl.ds(first, chunk)] = jnp.concatenate(
            [o.reshape(chunk, TILE, HD) for o in outputs], axis=1).astype(BF16)

    each(1, chunk, lambda k: q_copy(k).wait_recv())
    block(0)
    each(1, chunk, lambda k: r_copy(k).start())

    def far_block(index):
        first = index * chunk
        each(0, chunk, lambda i: q_copy(first + i).wait_recv())
        block(first)
        each(0, chunk, lambda i: r_copy(first + i).start())

    each(1, n // chunk, far_block)

    each(1, n, lambda k: p_copy(k).wait_recv())
    loads[5].wait()
    loads[6].wait()
    blocks = sk.shape[2] // HD

    def wide(row):
        return jnp.concatenate([jnp.broadcast_to(row, (2 * slots, HD))] * blocks, axis=1)

    def land(k, carry):
        notes = q_tiles[k].astype(F32)[notes_at:]
        child, child_length = wide(notes[:1]), wide(notes[1:2])
        arrived = pieces[k].astype(F32)
        out = []
        for j in range(BRANCHES):
            cache, length = carry[j]
            mine = child == (base + j).astype(F32)
            out.append((jnp.where(mine, arrived, cache), jnp.where(mine, child_length, length)))
        return tuple(out)

    shape = (2 * slots, sk.shape[2])
    landed = fold(0, n, land, tuple(
        (own_suffix(j), jnp.full(shape, len_ref[j].astype(F32))) for j in range(BRANCHES)))

    slot = lax.rem(lax.broadcasted_iota(jnp.int32, shape, 0), slots).astype(F32)
    nk_all, nv_all = nk[...].astype(F32), nv[...].astype(F32)
    caches = []
    for j in range(BRANCHES):
        cache, length = landed[j]
        fresh = jnp.concatenate([
            jnp.broadcast_to(nk_all[j:j + 1], (slots, shape[1])),
            jnp.broadcast_to(nv_all[j:j + 1], (slots, shape[1]))], axis=0)
        cache = jnp.where(slot == length, fresh, cache)
        ck[j] = cache[:slots].astype(BF16)
        cv[j] = cache[slots:].astype(BF16)
        caches.append(cache)

    parts = kv_local + 1
    keys_count = BRANCHES * slots
    row_id = lax.broadcasted_iota(jnp.int32, (parts * TILE, keys_count), 0)
    key_id = lax.broadcasted_iota(jnp.int32, (parts * TILE, keys_count), 1)
    key_length = jnp.where(
        key_id[:1] >= slots, landed[1][1][:1, :keys_count], landed[0][1][:1, :keys_count])
    live = jnp.logical_and(
        lax.rem(row_id, BRANCHES) == key_id // slots,
        lax.rem(key_id, slots).astype(F32) <= jnp.broadcast_to(key_length, row_id.shape))
    own_q = q_f32[...]
    own_scores, rest_scores = [], None
    owner = lax.broadcasted_iota(jnp.int32, (TILE, HD), 0) // BRANCHES
    for g in range(kv_local):
        keys = jnp.concatenate(
            [c[:slots, g * HD:(g + 1) * HD] for c in caches], axis=0).astype(BF16)
        q = jnp.concatenate(
            [own_q[g * TILE:(g + 1) * TILE], own_q[rest:notes_at]], axis=0).astype(BF16)
        s = lax.dot_general(q, keys, NT, preferred_element_type=F32) * scale
        own_scores.append(s[:TILE])
        rest_scores = s[TILE:] if g == 0 else jnp.where(
            owner[:, :keys_count] == g, s[TILE:], rest_scores)
    scores = jnp.concatenate(own_scores + [rest_scores], axis=0)
    row_max = jnp.max(jnp.where(live, scores, -jnp.inf), axis=1, keepdims=True)
    weights = jnp.where(live, jnp.exp(scores - row_max), 0.0)
    row_total = jnp.sum(weights, axis=1, keepdims=True)
    own_sums, rest_sum = [], None
    for g in range(kv_local):
        values = jnp.concatenate(
            [c[slots:, g * HD:(g + 1) * HD] for c in caches], axis=0).astype(BF16)
        w = jnp.concatenate(
            [weights[g * TILE:(g + 1) * TILE], weights[rest:notes_at]], axis=0).astype(BF16)
        o = jnp.dot(w, values, preferred_element_type=F32)
        own_sums.append(o[:TILE])
        rest_sum = o[TILE:] if g == 0 else jnp.where(owner == g, o[TILE:], rest_sum)
    own_sums.append(rest_sum)
    lane = lax.broadcasted_iota(jnp.int32, (TILE, HD), 1)
    own_top = jnp.zeros((TILE, HD), F32)
    own_total = jnp.ones((TILE, HD), F32)
    for g in range(parts):
        at = slice(g * TILE, (g + 1) * TILE)
        own_top = jnp.where(lane == g, row_max[at], own_top)
        own_total = jnp.where(lane == g, row_total[at], own_total)

    def lse_of(tile):
        terms = tile.astype(F32)[notes_at:]
        return terms + pltpu.roll(terms, HD - 16, 1) + pltpu.roll(terms, HD - 32, 1)

    each(1, n, lambda k: r_copy(k).wait_recv())
    best = fold(
        1, n, lambda k, m: jnp.maximum(m, lse_of(res_in[k])),
        jnp.maximum(own_top, lse_of(res_out[0])))

    def add(tile, carry):
        sums, total = carry
        factor = jnp.exp(lse_of(tile) - best)
        tile = tile.astype(F32)
        sums = tuple(
            s + tile[g * TILE:(g + 1) * TILE] * factor[:, g:g + 1] for g, s in enumerate(sums))
        return sums, total + factor

    own_factor = jnp.exp(own_top - best)
    carry = (
        tuple(s * own_factor[:, g:g + 1] for g, s in enumerate(own_sums)),
        own_total * own_factor)
    carry = add(res_out[0], carry)
    sums, total = fold(1, n, lambda k, c: add(res_in[k], c), carry)
    for g in range(parts):
        att_rows[g * TILE:(g + 1) * TILE, :] = sums[g] / total[:, g:g + 1]
    att[...] = jnp.concatenate(
        [att_rows[row_of(g, h):row_of(g, h) + BRANCHES, :]
         for g in range(kv_local) for h in range(GROUP)], axis=1).astype(BF16)

    def drain(k):
        q_copy(k).wait_send()
        p_copy(k).wait_send()
        r_copy(k).wait_send()

    each(1, n, drain)


def place(*refs):
    count = len(refs) // 2
    sems = refs[-1]
    copies = [
        pltpu.make_async_copy(refs[i], refs[count + i], sems.at[i]) for i in range(count)]
    for item in copies:
        item.start()
    for item in copies:
        item.wait()


def shards(n, *args):
    queries, prefix_keys, prefix_values, suffix_keys, suffix_values = args[:5]
    new_keys, new_values, suffix_lengths, fork_list = args[5:]
    slots, width = suffix_keys.shape[1:]
    kv_local = width // HD
    rows = (kv_local + 2) * TILE
    assert queries.shape[0] == BRANCHES and fork_list.shape[0] == 1
    assert n * BRANCHES <= 256 and rows % 16 == 0 and n & (n - 1) == 0
    dma = pltpu.SemaphoreType.DMA
    hbm_spec = pl.BlockSpec(memory_space=pltpu.HBM)
    smem_spec = pl.BlockSpec(memory_space=pltpu.SMEM)
    vmem_spec = pl.BlockSpec(memory_space=pltpu.VMEM)
    like = lambda x: pltpu.VMEM(x.shape, x.dtype)
    out_shape = (
        jax.ShapeDtypeStruct(queries.shape, BF16),
        jax.ShapeDtypeStruct(suffix_keys.shape, BF16),
        jax.ShapeDtypeStruct(suffix_values.shape, BF16),
    )
    results = pl.pallas_call(
        functools.partial(kernel, n),
        out_shape=out_shape,
        in_specs=[hbm_spec] * 7 + [smem_spec] * 2,
        out_specs=(vmem_spec,) * 3,
        scratch_shapes=[
            like(queries), like(prefix_keys), like(prefix_values), like(suffix_keys),
            like(suffix_values), like(new_keys), like(new_values),
            pltpu.VMEM((rows, HD), F32),
            pltpu.VMEM((n, rows, HD), BF16),
            pltpu.VMEM((n, 2 * slots, width), BF16),
            pltpu.VMEM((n, rows, HD), BF16),
            pltpu.VMEM((n, rows, HD), BF16),
            pltpu.VMEM((rows, HD), F32),
            dma((7,)),
        ] + [dma((n,))] * 6,
        compiler_params=pltpu.CompilerParams(
            collective_id=0, has_side_effects=True, vmem_limit_bytes=64 * 2**20),
    )(*args)
    return pl.pallas_call(
        place,
        out_shape=out_shape,
        in_specs=[hbm_spec] * 3,
        out_specs=(hbm_spec,) * 3,
        scratch_shapes=[dma((3,))],
        compiler_params=pltpu.CompilerParams(vmem_limit_bytes=64 * 2**20),
    )(*results)


def solution(mesh):
    return jax.shard_map(
        functools.partial(shards, mesh.shape["seq"]),
        mesh=mesh,
        in_specs=(
            P(("groups", "seq"), "mp"),
            P(("groups", "seq"), "mp"),
            P(("groups", "seq"), "mp"),
            P(("groups", "seq"), None, "mp"),
            P(("groups", "seq"), None, "mp"),
            P(("groups", "seq"), "mp"),
            P(("groups", "seq"), "mp"),
            P(("groups", "seq")),
            P(("groups", "seq"), None),
        ),
        out_specs=(
            P(("groups", "seq"), "mp"),
            P(("groups", "seq"), None, "mp"),
            P(("groups", "seq"), None, "mp"),
        ),
        check_vma=False,
    )
```

profile of v0, /device:TPU:0, one launch (start us, length us, event | category | flops | bytes accessed | tf_op | source)
XLA Modules:
  0.0 21.2 jit_solution(13934137645332120)
XLA Ops:
  0.6 18.1 %shard_map.112 = (bf16[2,2560]{1,0:T(2,128)(2,1)}, bf16[2,8,512]{2,1,0:T(8,128)(2,1)}, bf16[2,8,512]{2,1,0:T(8,128)(2,1)}) custom-call(bf16[2,2560]{1,0:T(2,128)(2,1)} %q_hbm.1, bf16[256,512]{1,0:T(8,128)(2,1)} %pk_hbm.1, bf16[256,512]{1,0:T(8,128)(2,1)} %pv_hbm.1, bf16[2,8,512]{2,1,0:T(8,128)(2,1)} %sk_hbm.1, bf16[2,8,512]{2,1,0:T(8,128)(2,1)} %sv_hbm.1, ...), custom_call_target="tpu_custom_call" | custom-call | tf_op jit(solution)/shard_map/pallas_call | solution.py:338
  18.8 2.4 %shard_map.113 = (bf16[2,2560]{1,0:T(2,128)(2,1)}, bf16[2,8,512]{2,1,0:T(8,128)(2,1)}, bf16[2,8,512]{2,1,0:T(8,128)(2,1)}) custom-call(bf16[2,2560]{1,0:T(2,128)(2,1)} %get-tuple-element.6.refs_0_, bf16[2,8,512]{2,1,0:T(8,128)(2,1)} %get-tuple-element.7.refs_1_, bf16[2,8,512]{2,1,0:T(8,128)(2,1)} %get-tuple-element.8.refs_2_), custom_call_target="tpu_custom_call" | custom-call | tf_op jit(solution)/shard_map/pallas_call | solution.py:357
where the time goes:
time: 21.5 us; the launch traced here: 21.2 us
  Pallas kernels  20.6 us (96%)
  between operations  0.64 us (3%)
    pallas_call x1, Pallas kernels, shards(): pl.pallas_call(functools.partial(kernel, n), out_shape=out_shape, in_spec...  18.1 us
    pallas_call x1, Pallas kernels, shards(): pl.pallas_call(place, out_shape=out_shape, in_specs=[hbm_spec] * 3, out_s...  2.43 us

commit v1 on v0

--- a/solution.py
+++ b/solution.py
@@ -43,9 +43,9 @@
 
 def kernel(
     n,
-    q_hbm, pk_hbm, pv_hbm, sk_hbm, sv_hbm, nk_hbm, nv_hbm, len_ref, fork_ref,
+    q_hbm, pk_hbm, pv_hbm, sk_hbm, sv_hbm, nk_hbm, nv_hbm, len_hbm, fork_hbm,
     att, ck, cv,
-    q_in, pk, pv, sk, sv, nk, nv,
+    q_in, pk, pv, sk, sv, nk, nv, len_ref, fork_ref,
     q_f32, q_tiles, pieces, res_out, res_in, att_rows,
     in_sem, q_send, q_recv, p_send, p_recv, r_send, r_recv,
 ):
@@ -73,14 +73,16 @@
         pltpu.make_async_copy(src, dst, in_sem.at[i])
         for i, (src, dst) in enumerate([
             (q_hbm, q_in), (sk_hbm, sk), (sv_hbm, sv), (pk_hbm, pk),
-            (pv_hbm, pv), (nk_hbm, nk), (nv_hbm, nv)])
+            (pv_hbm, pv), (nk_hbm, nk), (nv_hbm, nv), (len_hbm, len_ref), (fork_hbm, fork_ref)])
     ]
-    for load in loads:
-        load.start()
+    for i in (0, 7, 8, 1, 2, 3, 4, 5, 6):
+        loads[i].start()
 
     def row_of(g, h):
         return g * TILE + h * BRANCHES if h < GROUP - 1 else rest + g * BRANCHES
 
+    loads[7].wait()
+    loads[8].wait()
     parent = fork_ref[0, 0] - base
     parent_length = jnp.where(parent == 0, len_ref[0], len_ref[1])
     q_f32[notes_at:] = jnp.zeros((TILE, HD), F32)
@@ -327,7 +329,6 @@
     assert n * BRANCHES <= 256 and rows % 16 == 0 and n & (n - 1) == 0
     dma = pltpu.SemaphoreType.DMA
     hbm_spec = pl.BlockSpec(memory_space=pltpu.HBM)
-    smem_spec = pl.BlockSpec(memory_space=pltpu.SMEM)
     vmem_spec = pl.BlockSpec(memory_space=pltpu.VMEM)
     like = lambda x: pltpu.VMEM(x.shape, x.dtype)
     out_shape = (
@@ -338,29 +339,29 @@
     results = pl.pallas_call(
         functools.partial(kernel, n),
         out_shape=out_shape,
-        in_specs=[hbm_spec] * 7 + [smem_spec] * 2,
+        in_specs=[hbm_spec] * 9,
         out_specs=(vmem_spec,) * 3,
         scratch_shapes=[
             like(queries), like(prefix_keys), like(prefix_values), like(suffix_keys),
             like(suffix_values), like(new_keys), like(new_values),
+            pltpu.SMEM(suffix_lengths.shape, jnp.int32), pltpu.SMEM(fork_list.shape, jnp.int32),
             pltpu.VMEM((rows, HD), F32),
             pltpu.VMEM((n, rows, HD), BF16),
             pltpu.VMEM((n, 2 * slots, width), BF16),
             pltpu.VMEM((n, rows, HD), BF16),
             pltpu.VMEM((n, rows, HD), BF16),
             pltpu.VMEM((rows, HD), F32),
-            dma((7,)),
+            dma((9,)),
         ] + [dma((n,))] * 6,
         compiler_params=pltpu.CompilerParams(
-            collective_id=0, has_side_effects=True, vmem_limit_bytes=64 * 2**20),
-    )(*args)
+            collective_id=0, has_side_effects=True, vmem_limit_bytes=32 * 2**20),
+    )(*[pltpu.with_memory_space_constraint(x, pltpu.HBM) for x in args])
     return pl.pallas_call(
         place,
         out_shape=out_shape,
-        in_specs=[hbm_spec] * 3,
+        in_specs=[vmem_spec] * 3,
         out_specs=(hbm_spec,) * 3,
         scratch_shapes=[dma((3,))],
-        compiler_params=pltpu.CompilerParams(vmem_limit_bytes=64 * 2**20),
     )(*results)
 
 

time: 21.5 us -> 20.9 us (0.972)
  Pallas kernels: 20.6 us -> 18.3 us
  local copies, waits for them, and re-layouts: 0 us -> 1.78 us
    unnamed x0 -> x6, local copies, waits for them, and re-layouts: none -> 1.78 us
    pallas_call x1, Pallas kernels: 18.1 us -> 16.9 us  [shards(): pl.pallas_call(functools.partial(kernel, n), out_shape=out_shape, in_spec...]
    pallas_call x1, Pallas kernels: 2.43 us -> 1.39 us  [shards(): pl.pallas_call(place, out_shape=out_shape, in_specs=[vmem_spec] * 3, out_...]
where the time goes in v1:
time: 20.9 us; the launch traced here: 20.7 us
  Pallas kernels  18.3 us (88%)
  local copies, waits for them, and re-layouts  1.78 us (9%)
  between operations  0.65 us (3%)
    pallas_call x1, Pallas kernels, shards(): pl.pallas_call(functools.partial(kernel, n), out_shape=out_shape, in_spec...  16.9 us
    unnamed x6, local copies, waits for them, and re-layouts  1.78 us
    pallas_call x1, Pallas kernels, shards(): pl.pallas_call(place, out_shape=out_shape, in_specs=[vmem_spec] * 3, out_...  1.39 us

profile of v1, /device:TPU:0, one launch (start us, length us, event | category | flops | bytes accessed | tf_op | source)
XLA Modules:
  0.0 20.7 jit_solution(12593607656172986564)
XLA Ops:
  0.6 16.9 %shard_map.112 = (bf16[2,2560]{1,0:T(2,128)(2,1)S(1)}, bf16[2,8,512]{2,1,0:T(8,128)(2,1)S(1)}, bf16[2,8,512]{2,1,0:T(8,128)(2,1)S(1)}) custom-call(bf16[2,2560]{1,0:T(2,128)(2,1)} %q_hbm.1, bf16[256,512]{1,0:T(8,128)(2,1)} %pk_hbm.1, bf16[256,512]{1,0:T(8,128)(2,1)} %pv_hbm.1, bf16[2,8,512]{2,1,0:T(8,128)(2,1)} %sk_hbm.1, bf16[2,8,512]{2,1,0:T(8,128)(2,1)} %sv_hbm.1, ...), custom_call_target="tpu_custom_call" | custom-call | tf_op jit(solution)/shard_map/pallas_call | solution.py:339
  17.5 0.0 copy-start
  17.5 0.6 %copy-done = bf16[2,8,512]{2,1,0:T(8,128)(2,1)} copy-done((bf16[2,8,512]{2,1,0:T(8,128)(2,1)}, bf16[2,8,512]{2,1,0:T(8,128)(2,1)S(1)}, u32[]{:S(2)}) %copy-start) | copy-done | bytes 16408
  18.1 0.0 copy-start.1
  18.1 0.6 %copy-done.1 = bf16[2,8,512]{2,1,0:T(8,128)(2,1)} copy-done((bf16[2,8,512]{2,1,0:T(8,128)(2,1)}, bf16[2,8,512]{2,1,0:T(8,128)(2,1)S(1)}, u32[]{:S(2)}) %copy-start.1) | copy-done | bytes 16408
  18.7 0.0 copy-start.2
  18.7 0.6 %copy-done.2 = bf16[2,2560]{1,0:T(2,128)(2,1)} copy-done((bf16[2,2560]{1,0:T(2,128)(2,1)}, bf16[2,2560]{1,0:T(2,128)(2,1)S(1)}, u32[]{:S(2)}) %copy-start.2) | copy-done | bytes 10264
  19.3 1.4 %shard_map.113 = (bf16[2,2560]{1,0:T(2,128)(2,1)}, bf16[2,8,512]{2,1,0:T(8,128)(2,1)}, bf16[2,8,512]{2,1,0:T(8,128)(2,1)}) custom-call(bf16[2,2560]{1,0:T(2,128)(2,1)} %copy-done.2, bf16[2,8,512]{2,1,0:T(8,128)(2,1)} %copy-done, bf16[2,8,512]{2,1,0:T(8,128)(2,1)} %copy-done.1), custom_call_target="tpu_custom_call" | custom-call | tf_op jit(solution)/shard_map/pallas_call | solution.py:359
Async XLA Ops:
  17.5 0.6 %copy-start = (bf16[2,8,512]{2,1,0:T(8,128)(2,1)}, bf16[2,8,512]{2,1,0:T(8,128)(2,1)S(1)}, u32[]{:S(2)}) copy-start(bf16[2,8,512]{2,1,0:T(8,128)(2,1)S(1)} %get-tuple-element.7.refs_1_) | copy-start | bytes 49156
  18.1 0.6 %copy-start.1 = (bf16[2,8,512]{2,1,0:T(8,128)(2,1)}, bf16[2,8,512]{2,1,0:T(8,128)(2,1)S(1)}, u32[]{:S(2)}) copy-start(bf16[2,8,512]{2,1,0:T(8,128)(2,1)S(1)} %get-tuple-element.8.refs_2_) | copy-start | bytes 49156
  18.7 0.6 %copy-start.2 = (bf16[2,2560]{1,0:T(2,128)(2,1)}, bf16[2,2560]{1,0:T(2,128)(2,1)S(1)}, u32[]{:S(2)}) copy-start(bf16[2,2560]{1,0:T(2,128)(2,1)S(1)} %get-tuple-element.6.refs_0_) | copy-start | bytes 30724

commit v2 on v1

--- a/solution.py
+++ b/solution.py
@@ -109,6 +109,12 @@
     def p_copy(k):
         return copy(pieces.at[0], pieces.at[k], p_send, p_recv, k)
 
+    def p_pass(k):
+        return pltpu.make_async_remote_copy(
+            src_ref=pieces.at[k], dst_ref=pieces.at[k + 1],
+            send_sem=p_send.at[k + 1], recv_sem=p_recv.at[k + 1],
+            device_id=partner(1), device_id_type=MESH)
+
     def r_copy(k):
         return copy(res_out.at[k], res_in.at[k], r_send, r_recv, k)
 
@@ -126,7 +132,8 @@
 
     parent_b = jnp.full((2 * slots, sk.shape[2]), parent.astype(F32))
     pieces[0] = jnp.where(parent_b == 0.0, own_suffix(0), own_suffix(1)).astype(BF16)
-    far_first(lambda k: p_copy(k).start())
+    each(1, n // 2, lambda i: p_copy(n - 2 * i).start())
+    p_copy(1).start()
 
     loads[3].wait()
     loads[4].wait()
@@ -192,7 +199,13 @@
 
     each(1, n // chunk, far_block)
 
-    each(1, n, lambda k: p_copy(k).wait_recv())
+    def pass_on(i):
+        p_copy(2 * i).wait_recv()
+        p_pass(2 * i).start()
+
+    each(1, n // 2, pass_on)
+    p_copy(1).wait_recv()
+    each(1, n // 2, lambda i: p_pass(2 * i).wait_recv())
     loads[5].wait()
     loads[6].wait()
     blocks = sk.shape[2] // HD
@@ -302,10 +315,15 @@
 
     def drain(k):
         q_copy(k).wait_send()
-        p_copy(k).wait_send()
         r_copy(k).wait_send()
 
+    def drain_pieces(i):
+        p_copy(2 * i).wait_send()
+        p_pass(2 * i).wait_send()
+
     each(1, n, drain)
+    p_copy(1).wait_send()
+    each(1, n // 2, drain_pieces)
 
 
 def place(*refs):
@@ -362,6 +380,7 @@
         in_specs=[vmem_spec] * 3,
         out_specs=(hbm_spec,) * 3,
         scratch_shapes=[dma((3,))],
+        compiler_params=pltpu.CompilerParams(vmem_limit_bytes=2**20),
     )(*results)
 
 

time: 20.9 us -> 17.9 us (0.86)
  local copies, waits for them, and re-layouts: 1.78 us -> 0 us
  Pallas kernels: 18.3 us -> 17.1 us
    unnamed x6 -> x0, local copies, waits for them, and re-layouts: 1.78 us -> none
    pallas_call x1, Pallas kernels: 1.39 us -> 0.64 us  [shards(): pl.pallas_call(place, out_shape=out_shape, in_specs=[vmem_spec] * 3, out_...]
    pallas_call x1, Pallas kernels: 16.9 us -> 16.4 us  [shards(): pl.pallas_call(functools.partial(kernel, n), out_shape=out_shape, in_spec...]
where the time goes in v2:
time: 17.9 us; the launch traced here: 17.7 us
  Pallas kernels  17.1 us (96%)
  between operations  0.64 us (4%)
    pallas_call x1, Pallas kernels, shards(): pl.pallas_call(functools.partial(kernel, n), out_shape=out_shape, in_spec...  16.4 us
    pallas_call x1, Pallas kernels, shards(): pl.pallas_call(place, out_shape=out_shape, in_specs=[vmem_spec] * 3, out_...  0.64 us

profile of v2, /device:TPU:0, one launch (start us, length us, event | category | flops | bytes accessed | tf_op | source)
XLA Modules:
  0.0 17.7 jit_solution(14939633166185632791)
XLA Ops:
  0.6 16.4 %shard_map.112 = (bf16[2,2560]{1,0:T(2,128)(2,1)S(1)}, bf16[2,8,512]{2,1,0:T(8,128)(2,1)S(1)}, bf16[2,8,512]{2,1,0:T(8,128)(2,1)S(1)}) custom-call(bf16[2,2560]{1,0:T(2,128)(2,1)} %q_hbm.1, bf16[256,512]{1,0:T(8,128)(2,1)} %pk_hbm.1, bf16[256,512]{1,0:T(8,128)(2,1)} %pv_hbm.1, bf16[2,8,512]{2,1,0:T(8,128)(2,1)} %sk_hbm.1, bf16[2,8,512]{2,1,0:T(8,128)(2,1)} %sv_hbm.1, ...), custom_call_target="tpu_custom_call" | custom-call | tf_op jit(solution)/shard_map/pallas_call | solution.py:357
  17.1 0.6 %shard_map.113 = (bf16[2,2560]{1,0:T(2,128)(2,1)}, bf16[2,8,512]{2,1,0:T(8,128)(2,1)}, bf16[2,8,512]{2,1,0:T(8,128)(2,1)}) custom-call(bf16[2,2560]{1,0:T(2,128)(2,1)S(1)} %get-tuple-element.6.refs_0_, bf16[2,8,512]{2,1,0:T(8,128)(2,1)S(1)} %get-tuple-element.7.refs_1_, bf16[2,8,512]{2,1,0:T(8,128)(2,1)S(1)} %get-tuple-element.8.refs_2_), custom_call_target="tpu_custom_call" | custom-call | tf_op jit(solution)/shard_map/pallas_call | solution.py:377

commit v3 on v2

--- a/solution.py
+++ b/solution.py
@@ -96,6 +96,15 @@
             q_f32[row_of(g, h):row_of(g, h) + BRANCHES, :] = q_all[:, at:at + HD]
     q_tiles[0] = q_f32[...].astype(BF16)
 
+    loads[1].wait()
+    loads[2].wait()
+
+    def own_suffix(j):
+        return jnp.concatenate([sk[j].astype(F32), sv[j].astype(F32)], axis=0)
+
+    parent_b = jnp.full((2 * slots, sk.shape[2]), parent.astype(F32))
+    pieces[0] = jnp.where(parent_b == 0.0, own_suffix(0), own_suffix(1)).astype(BF16)
+
     pl.semaphore_wait(barrier, n - 1)
 
     def copy(src, dst, send, recv, k):
@@ -122,17 +131,8 @@
         each(chunk, n, body)
         each(1, chunk, body)
 
+    each(1, n // 2, lambda i: p_copy(n - 2 * i).start())
     far_first(lambda k: q_copy(k).start())
-
-    loads[1].wait()
-    loads[2].wait()
-
-    def own_suffix(j):
-        return jnp.concatenate([sk[j].astype(F32), sv[j].astype(F32)], axis=0)
-
-    parent_b = jnp.full((2 * slots, sk.shape[2]), parent.astype(F32))
-    pieces[0] = jnp.where(parent_b == 0.0, own_suffix(0), own_suffix(1)).astype(BF16)
-    each(1, n // 2, lambda i: p_copy(n - 2 * i).start())
     p_copy(1).start()
 
     loads[3].wait()
@@ -187,6 +187,11 @@
         res_out[pl.ds(first, chunk)] = jnp.concatenate(
             [o.reshape(chunk, TILE, HD) for o in outputs], axis=1).astype(BF16)
 
+    def pass_on(i):
+        p_copy(2 * i).wait_recv()
+        p_pass(2 * i).start()
+
+    each(1, n // 2, pass_on)
     each(1, chunk, lambda k: q_copy(k).wait_recv())
     block(0)
     each(1, chunk, lambda k: r_copy(k).start())
@@ -199,13 +204,6 @@
 
     each(1, n // chunk, far_block)
 
-    def pass_on(i):
-        p_copy(2 * i).wait_recv()
-        p_pass(2 * i).start()
-
-    each(1, n // 2, pass_on)
-    p_copy(1).wait_recv()
-    each(1, n // 2, lambda i: p_pass(2 * i).wait_recv())
     loads[5].wait()
     loads[6].wait()
     blocks = sk.shape[2] // HD
@@ -225,8 +223,12 @@
         return tuple(out)
 
     shape = (2 * slots, sk.shape[2])
-    landed = fold(0, n, land, tuple(
-        (own_suffix(j), jnp.full(shape, len_ref[j].astype(F32))) for j in range(BRANCHES)))
+    landed = tuple(
+        (own_suffix(j), jnp.full(shape, len_ref[j].astype(F32))) for j in range(BRANCHES))
+    landed = fold(0, n // 2, lambda i, c: land(2 * i, c), landed)
+    p_copy(1).wait_recv()
+    each(1, n // 2, lambda i: p_pass(2 * i).wait_recv())
+    landed = fold(0, n // 2, lambda i, c: land(2 * i + 1, c), landed)
 
     slot = lax.rem(lax.broadcasted_iota(jnp.int32, shape, 0), slots).astype(F32)
     nk_all, nv_all = nk[...].astype(F32), nv[...].astype(F32)
@@ -288,12 +290,10 @@
         terms = tile.astype(F32)[notes_at:]
         return terms + pltpu.roll(terms, HD - 16, 1) + pltpu.roll(terms, HD - 32, 1)
 
-    each(1, n, lambda k: r_copy(k).wait_recv())
-    best = fold(
-        1, n, lambda k, m: jnp.maximum(m, lse_of(res_in[k])),
-        jnp.maximum(own_top, lse_of(res_out[0])))
-
-    def add(tile, carry):
+    def highest(k, m):
+        return jnp.maximum(m, lse_of(res_in[k]))
+
+    def add(tile, best, carry):
         sums, total = carry
         factor = jnp.exp(lse_of(tile) - best)
         tile = tile.astype(F32)
@@ -301,12 +301,18 @@
             s + tile[g * TILE:(g + 1) * TILE] * factor[:, g:g + 1] for g, s in enumerate(sums))
         return sums, total + factor
 
-    own_factor = jnp.exp(own_top - best)
-    carry = (
-        tuple(s * own_factor[:, g:g + 1] for g, s in enumerate(own_sums)),
-        own_total * own_factor)
-    carry = add(res_out[0], carry)
-    sums, total = fold(1, n, lambda k, c: add(res_in[k], c), carry)
+    def scaled(factor, sums, total):
+        return tuple(s * factor[:, g:g + 1] for g, s in enumerate(sums)), total * factor
+
+    each(1, chunk, lambda k: r_copy(k).wait_recv())
+    near = fold(1, chunk, highest, jnp.maximum(own_top, lse_of(res_out[0])))
+    carry = scaled(jnp.exp(own_top - near), own_sums, own_total)
+    carry = add(res_out[0], near, carry)
+    carry = fold(1, chunk, lambda k, c: add(res_in[k], near, c), carry)
+    each(chunk, n, lambda k: r_copy(k).wait_recv())
+    best = fold(chunk, n, highest, near)
+    carry = scaled(jnp.exp(near - best), *carry)
+    sums, total = fold(chunk, n, lambda k, c: add(res_in[k], best, c), carry)
     for g in range(parts):
         att_rows[g * TILE:(g + 1) * TILE, :] = sums[g] / total[:, g:g + 1]
     att[...] = jnp.concatenate(

time: 17.9 us -> 18.4 us (1.028)
  Pallas kernels: 17.1 us -> 17.6 us
    pallas_call x1, Pallas kernels: 16.4 us -> 16.9 us  [shards(): pl.pallas_call(functools.partial(kernel, n), out_shape=out_shape, in_spec...]
where the time goes in v3:
time: 18.4 us; the launch traced here: 18.2 us
  Pallas kernels  17.6 us (96%)
  between operations  0.64 us (3%)
    pallas_call x1, Pallas kernels, shards(): pl.pallas_call(functools.partial(kernel, n), out_shape=out_shape, in_spec...  16.9 us
    pallas_call x1, Pallas kernels, shards(): pl.pallas_call(place, out_shape=out_shape, in_specs=[vmem_spec] * 3, out_...  0.64 us

profile of v3, /device:TPU:0, one launch (start us, length us, event | category | flops | bytes accessed | tf_op | source)
XLA Modules:
  0.0 18.2 jit_solution(378002939358517261)
XLA Ops:
  0.6 16.9 %shard_map.112 = (bf16[2,2560]{1,0:T(2,128)(2,1)S(1)}, bf16[2,8,512]{2,1,0:T(8,128)(2,1)S(1)}, bf16[2,8,512]{2,1,0:T(8,128)(2,1)S(1)}) custom-call(bf16[2,2560]{1,0:T(2,128)(2,1)} %q_hbm.1, bf16[256,512]{1,0:T(8,128)(2,1)} %pk_hbm.1, bf16[256,512]{1,0:T(8,128)(2,1)} %pv_hbm.1, bf16[2,8,512]{2,1,0:T(8,128)(2,1)} %sk_hbm.1, bf16[2,8,512]{2,1,0:T(8,128)(2,1)} %sv_hbm.1, ...), custom_call_target="tpu_custom_call" | custom-call | tf_op jit(solution)/shard_map/pallas_call | solution.py:363
  17.6 0.6 %shard_map.113 = (bf16[2,2560]{1,0:T(2,128)(2,1)}, bf16[2,8,512]{2,1,0:T(8,128)(2,1)}, bf16[2,8,512]{2,1,0:T(8,128)(2,1)}) custom-call(bf16[2,2560]{1,0:T(2,128)(2,1)S(1)} %get-tuple-element.6.refs_0_, bf16[2,8,512]{2,1,0:T(8,128)(2,1)S(1)} %get-tuple-element.7.refs_1_, bf16[2,8,512]{2,1,0:T(8,128)(2,1)S(1)} %get-tuple-element.8.refs_2_), custom_call_target="tpu_custom_call" | custom-call | tf_op jit(solution)/shard_map/pallas_call | solution.py:383

commit v4 on v3

--- a/solution.py
+++ b/solution.py
@@ -131,8 +131,8 @@
         each(chunk, n, body)
         each(1, chunk, body)
 
+    far_first(lambda k: q_copy(k).start())
     each(1, n // 2, lambda i: p_copy(n - 2 * i).start())
-    far_first(lambda k: q_copy(k).start())
     p_copy(1).start()
 
     loads[3].wait()
@@ -187,11 +187,6 @@
         res_out[pl.ds(first, chunk)] = jnp.concatenate(
             [o.reshape(chunk, TILE, HD) for o in outputs], axis=1).astype(BF16)
 
-    def pass_on(i):
-        p_copy(2 * i).wait_recv()
-        p_pass(2 * i).start()
-
-    each(1, n // 2, pass_on)
     each(1, chunk, lambda k: q_copy(k).wait_recv())
     block(0)
     each(1, chunk, lambda k: r_copy(k).start())
@@ -203,6 +198,12 @@
         each(0, chunk, lambda i: r_copy(first + i).start())
 
     each(1, n // chunk, far_block)
+
+    def pass_on(i):
+        p_copy(2 * i).wait_recv()
+        p_pass(2 * i).start()
+
+    each(1, n // 2, pass_on)
 
     loads[5].wait()
     loads[6].wait()

time: 18.4 us -> 17.9 us (0.973)
  Pallas kernels: 17.6 us -> 17.1 us
    pallas_call x1, Pallas kernels: 16.9 us -> 16.4 us  [shards(): pl.pallas_call(functools.partial(kernel, n), out_shape=out_shape, in_spec...]
where the time goes in v4:
time: 17.9 us; the launch traced here: 17.7 us
  Pallas kernels  17.1 us (96%)
  between operations  0.64 us (4%)
    pallas_call x1, Pallas kernels, shards(): pl.pallas_call(functools.partial(kernel, n), out_shape=out_shape, in_spec...  16.4 us
    pallas_call x1, Pallas kernels, shards(): pl.pallas_call(place, out_shape=out_shape, in_specs=[vmem_spec] * 3, out_...  0.64 us

profile of v4, /device:TPU:0, one launch (start us, length us, event | category | flops | bytes accessed | tf_op | source)
XLA Modules:
  0.0 17.7 jit_solution(15471124182356474494)
XLA Ops:
  0.6 16.4 %shard_map.112 = (bf16[2,2560]{1,0:T(2,128)(2,1)S(1)}, bf16[2,8,512]{2,1,0:T(8,128)(2,1)S(1)}, bf16[2,8,512]{2,1,0:T(8,128)(2,1)S(1)}) custom-call(bf16[2,2560]{1,0:T(2,128)(2,1)} %q_hbm.1, bf16[256,512]{1,0:T(8,128)(2,1)} %pk_hbm.1, bf16[256,512]{1,0:T(8,128)(2,1)} %pv_hbm.1, bf16[2,8,512]{2,1,0:T(8,128)(2,1)} %sk_hbm.1, bf16[2,8,512]{2,1,0:T(8,128)(2,1)} %sv_hbm.1, ...), custom_call_target="tpu_custom_call" | custom-call | tf_op jit(solution)/shard_map/pallas_call | solution.py:364
  17.1 0.6 %shard_map.113 = (bf16[2,2560]{1,0:T(2,128)(2,1)}, bf16[2,8,512]{2,1,0:T(8,128)(2,1)}, bf16[2,8,512]{2,1,0:T(8,128)(2,1)}) custom-call(bf16[2,2560]{1,0:T(2,128)(2,1)S(1)} %get-tuple-element.6.refs_0_, bf16[2,8,512]{2,1,0:T(8,128)(2,1)S(1)} %get-tuple-element.7.refs_1_, bf16[2,8,512]{2,1,0:T(8,128)(2,1)S(1)} %get-tuple-element.8.refs_2_), custom_call_target="tpu_custom_call" | custom-call | tf_op jit(solution)/shard_map/pallas_call | solution.py:384

commit v5 on v4

--- a/solution.py
+++ b/solution.py
@@ -191,6 +191,12 @@
     block(0)
     each(1, chunk, lambda k: r_copy(k).start())
 
+    def pass_on(i):
+        p_copy(2 * i).wait_recv()
+        p_pass(2 * i).start()
+
+    each(1, n // 2, pass_on)
+
     def far_block(index):
         first = index * chunk
         each(0, chunk, lambda i: q_copy(first + i).wait_recv())
@@ -198,12 +204,6 @@
         each(0, chunk, lambda i: r_copy(first + i).start())
 
     each(1, n // chunk, far_block)
-
-    def pass_on(i):
-        p_copy(2 * i).wait_recv()
-        p_pass(2 * i).start()
-
-    each(1, n // 2, pass_on)
 
     loads[5].wait()
     loads[6].wait()

time: 17.9 us -> 17.9 us (level)
  no operation moved by 1% of the time
where the time goes in v5:
time: 17.9 us; the launch traced here: 17.7 us
  Pallas kernels  17.1 us (96%)
  between operations  0.64 us (4%)
    pallas_call x1, Pallas kernels, shards(): pl.pallas_call(functools.partial(kernel, n), out_shape=out_shape, in_spec...  16.4 us
    pallas_call x1, Pallas kernels, shards(): pl.pallas_call(place, out_shape=out_shape, in_specs=[vmem_spec] * 3, out_...  0.64 us

profile of v5, /device:TPU:0, one launch (start us, length us, event | category | flops | bytes accessed | tf_op | source)
XLA Modules:
  0.0 17.7 jit_solution(9315616258540984513)
XLA Ops:
  0.6 16.4 %shard_map.112 = (bf16[2,2560]{1,0:T(2,128)(2,1)S(1)}, bf16[2,8,512]{2,1,0:T(8,128)(2,1)S(1)}, bf16[2,8,512]{2,1,0:T(8,128)(2,1)S(1)}) custom-call(bf16[2,2560]{1,0:T(2,128)(2,1)} %q_hbm.1, bf16[256,512]{1,0:T(8,128)(2,1)} %pk_hbm.1, bf16[256,512]{1,0:T(8,128)(2,1)} %pv_hbm.1, bf16[2,8,512]{2,1,0:T(8,128)(2,1)} %sk_hbm.1, bf16[2,8,512]{2,1,0:T(8,128)(2,1)} %sv_hbm.1, ...), custom_call_target="tpu_custom_call" | custom-call | tf_op jit(solution)/shard_map/pallas_call | solution.py:364
  17.1 0.6 %shard_map.113 = (bf16[2,2560]{1,0:T(2,128)(2,1)}, bf16[2,8,512]{2,1,0:T(8,128)(2,1)}, bf16[2,8,512]{2,1,0:T(8,128)(2,1)}) custom-call(bf16[2,2560]{1,0:T(2,128)(2,1)S(1)} %get-tuple-element.6.refs_0_, bf16[2,8,512]{2,1,0:T(8,128)(2,1)S(1)} %get-tuple-element.7.refs_1_, bf16[2,8,512]{2,1,0:T(8,128)(2,1)S(1)} %get-tuple-element.8.refs_2_), custom_call_target="tpu_custom_call" | custom-call | tf_op jit(solution)/shard_map/pallas_call | solution.py:384
